TPU v7x, 256 devices: a whole 4x4x8 slice. The times are simulated.
256 devices in a mesh: gx: 32 (over y, x, core), gy: 8 (over z).
Axes of the slice: x: 4, y: 4, z: 8, core: 2. Of those that a mesh axis runs over, the one named last changes fastest.
Arguments:
- probes: float32 [64, 64, 64, 128], P(None, 'gx', 'gy'), may hold values from -6 to 6
- conduct: float32 [64, 64, 128], P('gx', 'gy'), may hold values from 0.25 to 2
- storage: float32 [64, 64, 128], P('gx', 'gy'), may hold values from 0.5 to 2
Outputs:
- basis: float32 [64, 64, 64, 128], P(None, 'gx', 'gy')
- factor: float32 [64, 64], replicated
All inputs are finite; a program needn't handle non-finite values.
Results may differ from a plain program's by a relative error of at most 0.00005.
Values sent between devices are 32-bit elements; how exact they have to be, the bound alone decides.
No kernel may reach another device: no remote copies, remote signals or barrier semaphores. Data moves between devices by JAX's collectives and lax.ppermute only.
A program may use at most 64 MiB of HBM per device.

v0:
```python
import math

import jax
import jax.numpy as jnp
from jax import lax
from jax.sharding import PartitionSpec as P

STEPS = 8


time_step = 0.07
prior_weight = 0.5


def with_halo(array, sides, width):
    for axis, dim in sides:
        count, length = (lax.axis_size(axis), array.shape[dim])
        up = [(i, (i + 1) % count) for i in range(count - 1)]
        down = [(j, i) for i, j in up]
        last = lax.slice_in_dim(array, length - width, length, axis=dim)
        initial = lax.slice_in_dim(array, 0, width, axis=dim)
        before = lax.ppermute(last, axis, up)
        after = lax.ppermute(initial, axis, down)
        array = jnp.concatenate([before, array, after], axis=dim)
    return array


def laplace_inner(padded):
    centre = padded[:, 1:-1, 1:-1, :]
    zero_plane = jnp.zeros_like(centre[..., :1])
    above = jnp.concatenate([centre[..., 1:], zero_plane], axis=3)
    below = jnp.concatenate([zero_plane, centre[..., :-1]], axis=3)
    beside = padded[:, 2:, 1:-1, :] + padded[:, :-2, 1:-1, :]
    beside = beside + padded[:, 1:-1, 2:, :] + padded[:, 1:-1, :-2, :]
    return 6.0 * centre - (beside + above + below)


def shards(probes, conduct, storage):
    num_probes, local_x, local_y, depth_z = probes.shape
    source = time_step * storage[None] * probes
    conduct_pad = with_halo(conduct, (("gx", 0), ("gy", 1)), 1)
    forward = source
    for sweep in range(STEPS):
        padded_state = with_halo(forward, (("gx", 1), ("gy", 2)), 1)
        forward = forward - time_step * laplace_inner(conduct_pad[None] * padded_state) + source
    costate = forward
    summed = forward
    for sweep in range(STEPS):
        padded_costate = with_halo(costate, (("gx", 1), ("gy", 2)), 1)
        costate = costate - time_step * conduct[None] * laplace_inner(padded_costate)
        summed = summed + costate
    response = time_step * storage[None] * summed + prior_weight * probes
    flat = response.reshape(num_probes, -1)
    local_gram = jnp.dot(flat, flat.T, precision=lax.Precision.HIGHEST)
    total_gram = lax.psum(local_gram, ("gx", "gy"))
    upper = jnp.linalg.cholesky(total_gram).T
    solved = jax.scipy.linalg.solve_triangular(upper.T, flat, lower=True)
    scale = math.sqrt(local_x * lax.axis_size("gx") * local_y * lax.axis_size("gy") * depth_z)
    return ((solved * scale).reshape(probes.shape), upper / scale)


def solution(mesh):
    placed = (P(None, "gx", "gy", None), P("gx", "gy", None), P("gx", "gy", None))
    return jax.shard_map(
        shards,
        mesh=mesh,
        in_specs=placed,
        out_specs=(P(None, "gx", "gy", None), P()),
        check_vma=False,
    )
```

profile of v0, /device:TPU:2, one launch (start us, length us, event | category | flops | bytes accessed | tf_op | source)
XLA Modules:
  0.0 470.5 jit_solution(4845443400320195139)
XLA Ops:
  17.3 3.7 collective-permute-start.6
  22.3 4.5 collective-permute-start.2
  28.2 4.2 collective-permute-done.3
  36.1 3.5 collective-permute-start.9
  43.5 4.8 %collective-permute-start.10 = (f32[64,4,1,128]{3,0,2,1:T(8,128)S(1)}, f32[64,4,1,128]{3,0,2,1:T(8,128)S(1)}, u32[]{:S(2)}, u32[]{:S(2)}) collective-permute-start(f32[64,4,1,128]{3,0,2,1:T(8,128)S(1)} %get-tuple-element.52), channel_id=1, source_target_pairs={{0,1},{1,2},{2,3},{3,4},{4,5},{5,6},{6,7},{8,9},{9,10},{10,11},{11... | collective-permute-start | bytes 393224 | tf_op jit(solution)/shard_map/ppermute | solution.py:22
  51.5 5.6 %collective-permute-done.11 = f32[64,4,1,128]{3,0,2,1:T(8,128)S(1)} collective-permute-done((f32[64,4,1,128]{3,0,2,1:T(8,128)S(1)}, f32[64,4,1,128]{3,0,2,1:T(8,128)S(1)}, u32[]{:S(2)}, u32[]{:S(2)}) %collective-permute-start.11) | collective-permute-done | bytes 131104 | tf_op jit(solution)/shard_map/ppermute | solution.py:23
  67.6 5.1 %collective-permute-start.14 = (f32[64,4,1,128]{3,0,2,1:T(8,128)S(1)}, f32[64,4,1,128]{3,0,2,1:T(8,128)S(1)}, u32[]{:S(2)}, u32[]{:S(2)}) collective-permute-start(f32[64,4,1,128]{3,0,2,1:T(8,128)S(1)} %get-tuple-element.50), channel_id=1, source_target_pairs={{0,1},{1,2},{2,3},{3,4},{4,5},{5,6},{6,7},{8,9},{9,10},{10,11},{11... | collective-permute-start | bytes 393224 | tf_op jit(solution)/shard_map/ppermute | solution.py:22
  76.2 5.0 %collective-permute-done.15 = f32[64,4,1,128]{3,0,2,1:T(8,128)S(1)} collective-permute-done((f32[64,4,1,128]{3,0,2,1:T(8,128)S(1)}, f32[64,4,1,128]{3,0,2,1:T(8,128)S(1)}, u32[]{:S(2)}, u32[]{:S(2)}) %collective-permute-start.15) | collective-permute-done | bytes 131104 | tf_op jit(solution)/shard_map/ppermute | solution.py:23
  84.2 3.6 collective-permute-start.17
  91.8 3.6 collective-permute-start.18
  97.9 4.4 collective-permute-done.19
  118.4 4.4 collective-permute-done.23
  123.8 5.2 %collective-permute-start.24 = (f32[64,1,8,128]{3,0,2,1:T(8,128)S(1)}, f32[64,1,8,128]{3,0,2,1:T(8,128)S(1)}, u32[]{:S(2)}, u32[]{:S(2)}) collective-permute-start(f32[64,1,8,128]{3,0,2,1:T(8,128)S(1)} %get-tuple-element.92), channel_id=1, source_target_pairs={{0,8},{8,16},{16,24},{24,32},{32,40},{40,48},{48,56},{56,64},{64,7... | collective-permute-start | bytes 786440 | tf_op jit(solution)/shard_map/ppermute | solution.py:22
  134.8 3.4 collective-permute-start.26
  140.7 4.4 collective-permute-done.27
  146.2 5.5 %collective-permute-start.28 = (f32[64,1,8,128]{3,0,2,1:T(8,128)S(1)}, f32[64,1,8,128]{3,0,2,1:T(8,128)S(1)}, u32[]{:S(2)}, u32[]{:S(2)}) collective-permute-start(f32[64,1,8,128]{3,0,2,1:T(8,128)S(1)} %get-tuple-element.90), channel_id=1, source_target_pairs={{0,8},{8,16},{16,24},{24,32},{32,40},{40,48},{48,56},{56,64},{64,7... | collective-permute-start | bytes 786440 | tf_op jit(solution)/shard_map/ppermute | solution.py:22
  153.8 3.6 collective-permute-done.29
  163.4 4.4 collective-permute-done.31
  168.8 5.5 %collective-permute-start.32 = (f32[64,1,8,128]{3,0,2,1:T(8,128)S(1)}, f32[64,1,8,128]{3,0,2,1:T(8,128)S(1)}, u32[]{:S(2)}, u32[]{:S(2)}) collective-permute-start(f32[64,1,8,128]{3,0,2,1:T(8,128)S(1)} %get-tuple-element.88), channel_id=1, source_target_pairs={{0,8},{8,16},{16,24},{24,32},{32,40},{40,48},{48,56},{56,64},{64,7... | collective-permute-start | bytes 786440 | tf_op jit(solution)/shard_map/ppermute | solution.py:22
  176.5 3.6 collective-permute-done.33
  186.0 4.4 collective-permute-done.35
  191.4 5.5 %collective-permute-start.37 = (f32[64,1,8,128]{3,0,2,1:T(8,128)S(1)}, f32[64,1,8,128]{3,0,2,1:T(8,128)S(1)}, u32[]{:S(2)}, u32[]{:S(2)}) collective-permute-start(f32[64,1,8,128]{3,0,2,1:T(8,128)S(1)} %get-tuple-element.86), channel_id=1, source_target_pairs={{0,8},{8,16},{16,24},{24,32},{32,40},{40,48},{48,56},{56,64},{64,7... | collective-permute-start | bytes 786440 | tf_op jit(solution)/shard_map/ppermute | solution.py:22
  199.1 3.6 collective-permute-done.36
  204.0 4.6 collective-permute-start.39
  211.5 6.0 %collective-permute-start.41 = (f32[64,1,8,128]{3,0,2,1:T(8,128)S(1)}, f32[64,1,8,128]{3,0,2,1:T(8,128)S(1)}, u32[]{:S(2)}, u32[]{:S(2)}) collective-permute-start(f32[64,1,8,128]{3,0,2,1:T(8,128)S(1)} %get-tuple-element.82), channel_id=1, source_target_pairs={{0,8},{8,16},{16,24},{24,32},{32,40},{40,48},{48,56},{56,64},{64,7... | collective-permute-start | bytes 786440 | tf_op jit(solution)/shard_map/ppermute | solution.py:22
  219.5 3.9 collective-permute-done.40
  224.7 4.7 collective-permute-start.43
  232.3 6.3 %collective-permute-start.45 = (f32[64,1,8,128]{3,0,2,1:T(8,128)S(1)}, f32[64,1,8,128]{3,0,2,1:T(8,128)S(1)}, u32[]{:S(2)}, u32[]{:S(2)}) collective-permute-start(f32[64,1,8,128]{3,0,2,1:T(8,128)S(1)} %get-tuple-element.78), channel_id=1, source_target_pairs={{0,8},{8,16},{16,24},{24,32},{32,40},{40,48},{48,56},{56,64},{64,7... | collective-permute-start | bytes 786440 | tf_op jit(solution)/shard_map/ppermute | solution.py:22
  240.5 3.9 collective-permute-done.44
  245.7 4.9 %collective-permute-start.47 = (f32[64,4,1,128]{3,0,2,1:T(8,128)S(1)}, f32[64,4,1,128]{3,0,2,1:T(8,128)S(1)}, u32[]{:S(2)}, u32[]{:S(2)}) collective-permute-start(f32[64,4,1,128]{3,0,2,1:T(8,128)S(1)} %get-tuple-element.35), channel_id=1, source_target_pairs={{0,1},{1,2},{2,3},{3,4},{4,5},{5,6},{6,7},{8,9},{9,10},{10,11},{11... | collective-permute-start | bytes 393224 | tf_op jit(solution)/shard_map/ppermute | solution.py:22
  253.5 6.3 %collective-permute-start.49 = (f32[64,1,8,128]{3,0,2,1:T(8,128)S(1)}, f32[64,1,8,128]{3,0,2,1:T(8,128)S(1)}, u32[]{:S(2)}, u32[]{:S(2)}) collective-permute-start(f32[64,1,8,128]{3,0,2,1:T(8,128)S(1)} %get-tuple-element.74), channel_id=1, source_target_pairs={{0,8},{8,16},{16,24},{24,32},{32,40},{40,48},{48,56},{56,64},{64,7... | collective-permute-start | bytes 786440 | tf_op jit(solution)/shard_map/ppermute | solution.py:22
  261.8 3.9 collective-permute-done.48
  266.9 4.7 collective-permute-start.51
  274.5 6.3 %collective-permute-start.53 = (f32[64,1,8,128]{3,0,2,1:T(8,128)S(1)}, f32[64,1,8,128]{3,0,2,1:T(8,128)S(1)}, u32[]{:S(2)}, u32[]{:S(2)}) collective-permute-start(f32[64,1,8,128]{3,0,2,1:T(8,128)S(1)} %get-tuple-element.70), channel_id=1, source_target_pairs={{0,8},{8,16},{16,24},{24,32},{32,40},{40,48},{48,56},{56,64},{64,7... | collective-permute-start | bytes 786440 | tf_op jit(solution)/shard_map/ppermute | solution.py:22
  282.8 3.9 collective-permute-done.52
  288.0 4.7 collective-permute-start.55
  295.6 6.0 %collective-permute-start.57 = (f32[64,1,8,128]{3,0,2,1:T(8,128)S(1)}, f32[64,1,8,128]{3,0,2,1:T(8,128)S(1)}, u32[]{:S(2)}, u32[]{:S(2)}) collective-permute-start(f32[64,1,8,128]{3,0,2,1:T(8,128)S(1)} %get-tuple-element.66), channel_id=1, source_target_pairs={{0,8},{8,16},{16,24},{24,32},{32,40},{40,48},{48,56},{56,64},{64,7... | collective-permute-start | bytes 786440 | tf_op jit(solution)/shard_map/ppermute | solution.py:22
  303.6 3.9 collective-permute-done.56
  308.7 5.5 %collective-permute-start.59 = (f32[64,4,1,128]{3,0,2,1:T(8,128)S(1)}, f32[64,4,1,128]{3,0,2,1:T(8,128)S(1)}, u32[]{:S(2)}, u32[]{:S(2)}) collective-permute-start(f32[64,4,1,128]{3,0,2,1:T(8,128)S(1)} %get-tuple-element.29), channel_id=1, source_target_pairs={{0,1},{1,2},{2,3},{3,4},{4,5},{5,6},{6,7},{8,9},{9,10},{10,11},{11... | collective-permute-start | bytes 393224 | tf_op jit(solution)/shard_map/ppermute | solution.py:22
  317.2 5.8 %collective-permute-start.61 = (f32[64,1,8,128]{3,0,2,1:T(8,128)S(1)}, f32[64,1,8,128]{3,0,2,1:T(8,128)S(1)}, u32[]{:S(2)}, u32[]{:S(2)}) collective-permute-start(f32[64,1,8,128]{3,0,2,1:T(8,128)S(1)} %get-tuple-element.62), channel_id=1, source_target_pairs={{0,8},{8,16},{16,24},{24,32},{32,40},{40,48},{48,56},{56,64},{64,7... | collective-permute-start | bytes 786440 | tf_op jit(solution)/shard_map/ppermute | solution.py:22
  324.9 3.9 collective-permute-done.60
  330.1 6.2 %collective-permute-start.63 = (f32[64,4,1,128]{3,0,2,1:T(8,128)S(1)}, f32[64,4,1,128]{3,0,2,1:T(8,128)S(1)}, u32[]{:S(2)}, u32[]{:S(2)}) collective-permute-start(f32[64,4,1,128]{3,0,2,1:T(8,128)S(1)} %get-tuple-element.27), channel_id=1, source_target_pairs={{0,1},{1,2},{2,3},{3,4},{4,5},{5,6},{6,7},{8,9},{9,10},{10,11},{11... | collective-permute-start | bytes 393224 | tf_op jit(solution)/shard_map/ppermute | solution.py:22
  339.2 5.8 %collective-permute-start.65 = (f32[64,1,8,128]{3,0,2,1:T(8,128)S(1)}, f32[64,1,8,128]{3,0,2,1:T(8,128)S(1)}, u32[]{:S(2)}, u32[]{:S(2)}) collective-permute-start(f32[64,1,8,128]{3,0,2,1:T(8,128)S(1)} %get-tuple-element.58), channel_id=1, source_target_pairs={{0,8},{8,16},{16,24},{24,32},{32,40},{40,48},{48,56},{56,64},{64,7... | collective-permute-start | bytes 786440 | tf_op jit(solution)/shard_map/ppermute | solution.py:22
  346.9 3.9 collective-permute-done.64
  352.0 6.2 %collective-permute-start.67 = (f32[64,4,1,128]{3,0,2,1:T(8,128)S(1)}, f32[64,4,1,128]{3,0,2,1:T(8,128)S(1)}, u32[]{:S(2)}, u32[]{:S(2)}) collective-permute-start(f32[64,4,1,128]{3,0,2,1:T(8,128)S(1)} %get-tuple-element.25), channel_id=1, source_target_pairs={{0,1},{1,2},{2,3},{3,4},{4,5},{5,6},{6,7},{8,9},{9,10},{10,11},{11... | collective-permute-start | bytes 393224 | tf_op jit(solution)/shard_map/ppermute | solution.py:22
  362.5 93.5 %psum.7 = f32[64,64]{0,1:T(8,128)S(1)} all-reduce(f32[64,64]{0,1:T(8,128)S(1)} %convolution_bitcast_fusion), channel_id=1, replica_groups=mesh['gx'=32,'gy'=8] {'gx','gy'}, use_global_device_ids=true, to_apply=%region_0.0 | all-reduce | flops 4096 | bytes 32768 | tf_op jit(solution)/shard_map/psum | solution.py:55
  456.0 5.8 %cholesky.16 = f32[64,64]{1,0:T(8,128)S(1)} custom-call(f32[64,64]{1,0:T(8,128)S(1)} %fusion.117), custom_call_target="Cholesky" | custom-call | tf_op jit(solution)/shard_map/jit(cholesky)/cholesky | solution.py:56
  463.9 4.9 %custom-call.7 = f32[1,64,64]{1,2,0:T(8,128)S(1)} custom-call(f32[1,64,64]{2,1,0:T(8,128)S(1)} %get-tuple-element.105), custom_call_target="InvertDiagBlocksLowerTriangular" | custom-call | tf_op jit(solution)/shard_map/jit(_solve_triangular)/triangular_solve | solution.py:57
  (185 shorter events, 152.1 us)
Async XLA Ops:
  1.4 12.1 %collective-permute-start.1 = (f32[1,8,128]{2,1,0:T(8,128)S(1)}, f32[1,8,128]{2,1,0:T(8,128)S(1)}, u32[]{:S(2)}, u32[]{:S(2)}) collective-permute-start(f32[1,8,128]{2,1,0:T(8,128)S(1)} %get-tuple-element.110), channel_id=1, source_target_pairs={{8,0},{16,8},{24,16},{32,24},{40,32},{48,40},{56,48},{64,56},{72,6... | collective-permute-start | bytes 12296 | tf_op jit(solution)/shard_map/ppermute | solution.py:23
  3.3 10.1 %collective-permute-start = (f32[1,8,128]{2,1,0:T(8,128)S(1)}, f32[1,8,128]{2,1,0:T(8,128)S(1)}, u32[]{:S(2)}, u32[]{:S(2)}) collective-permute-start(f32[1,8,128]{2,1,0:T(8,128)S(1)} %get-tuple-element.111), channel_id=1, source_target_pairs={{0,8},{8,16},{16,24},{24,32},{32,40},{40,48},{48,56},{56,64},{64,7... | collective-permute-start | bytes 12296 | tf_op jit(solution)/shard_map/ppermute | solution.py:22
  7.7 7.8 %collective-permute-start.4 = (f32[64,1,8,128]{3,0,2,1:T(8,128)S(1)}, f32[64,1,8,128]{3,0,2,1:T(8,128)S(1)}, u32[]{:S(2)}, u32[]{:S(2)}) collective-permute-start(f32[64,1,8,128]{3,0,2,1:T(8,128)S(1)} %get-tuple-element.102), channel_id=1, source_target_pairs={{0,8},{8,16},{16,24},{24,32},{32,40},{40,48},{48,56},{56,64},{64,7... | collective-permute-start | bytes 786440 | tf_op jit(solution)/shard_map/ppermute | solution.py:22
  17.3 15.0 %collective-permute-start.6 = (f32[64,4,1,128]{3,0,2,1:T(8,128)S(1)}, f32[64,4,1,128]{3,0,2,1:T(8,128)S(1)}, u32[]{:S(2)}, u32[]{:S(2)}) collective-permute-start(f32[64,4,1,128]{3,0,2,1:T(8,128)S(1)} %get-tuple-element.54), channel_id=1, source_target_pairs={{0,1},{1,2},{2,3},{3,4},{4,5},{5,6},{6,7},{8,9},{9,10},{10,11},{11... | collective-permute-start | bytes 393224 | tf_op jit(solution)/shard_map/ppermute | solution.py:22
  21.0 11.4 %collective-permute-start.7 = (f32[64,4,1,128]{3,0,2,1:T(8,128)S(1)}, f32[64,4,1,128]{3,0,2,1:T(8,128)S(1)}, u32[]{:S(2)}, u32[]{:S(2)}) collective-permute-start(f32[64,4,1,128]{3,0,2,1:T(8,128)S(1)} %get-tuple-element.55), channel_id=1, source_target_pairs={{1,0},{2,1},{3,2},{4,3},{5,4},{6,5},{7,6},{9,8},{10,9},{11,10},{12... | collective-permute-start | bytes 393224 | tf_op jit(solution)/shard_map/ppermute | solution.py:23
  34.1 7.7 %collective-permute-start.8 = (f32[64,1,8,128]{3,0,2,1:T(8,128)S(1)}, f32[64,1,8,128]{3,0,2,1:T(8,128)S(1)}, u32[]{:S(2)}, u32[]{:S(2)}) collective-permute-start(f32[64,1,8,128]{3,0,2,1:T(8,128)S(1)} %get-tuple-element.100), channel_id=1, source_target_pairs={{0,8},{8,16},{16,24},{24,32},{32,40},{40,48},{48,56},{56,64},{64,7... | collective-permute-start | bytes 786440 | tf_op jit(solution)/shard_map/ppermute | solution.py:22
  36.1 7.4 %collective-permute-start.9 = (f32[64,1,8,128]{3,0,2,1:T(8,128)S(1)}, f32[64,1,8,128]{3,0,2,1:T(8,128)S(1)}, u32[]{:S(2)}, u32[]{:S(2)}) collective-permute-start(f32[64,1,8,128]{3,0,2,1:T(8,128)S(1)} %get-tuple-element.101), channel_id=1, source_target_pairs={{8,0},{16,8},{24,16},{32,24},{40,32},{48,40},{56,48},{64,56},{72,6... | collective-permute-start | bytes 786440 | tf_op jit(solution)/shard_map/ppermute | solution.py:23
  43.5 8.0 %collective-permute-start.10 = (f32[64,4,1,128]{3,0,2,1:T(8,128)S(1)}, f32[64,4,1,128]{3,0,2,1:T(8,128)S(1)}, u32[]{:S(2)}, u32[]{:S(2)}) collective-permute-start(f32[64,4,1,128]{3,0,2,1:T(8,128)S(1)} %get-tuple-element.52), channel_id=1, source_target_pairs={{0,1},{1,2},{2,3},{3,4},{4,5},{5,6},{6,7},{8,9},{9,10},{10,11},{11... | collective-permute-start | bytes 393224 | tf_op jit(solution)/shard_map/ppermute | solution.py:22
  48.4 8.7 %collective-permute-start.11 = (f32[64,4,1,128]{3,0,2,1:T(8,128)S(1)}, f32[64,4,1,128]{3,0,2,1:T(8,128)S(1)}, u32[]{:S(2)}, u32[]{:S(2)}) collective-permute-start(f32[64,4,1,128]{3,0,2,1:T(8,128)S(1)} %get-tuple-element.53), channel_id=1, source_target_pairs={{1,0},{2,1},{3,2},{4,3},{5,4},{6,5},{7,6},{9,8},{10,9},{11,10},{12... | collective-permute-start | bytes 393224 | tf_op jit(solution)/shard_map/ppermute | solution.py:23
  58.2 7.7 %collective-permute-start.12 = (f32[64,1,8,128]{3,0,2,1:T(8,128)S(1)}, f32[64,1,8,128]{3,0,2,1:T(8,128)S(1)}, u32[]{:S(2)}, u32[]{:S(2)}) collective-permute-start(f32[64,1,8,128]{3,0,2,1:T(8,128)S(1)} %get-tuple-element.98), channel_id=1, source_target_pairs={{0,8},{8,16},{16,24},{24,32},{32,40},{40,48},{48,56},{56,64},{64,7... | collective-permute-start | bytes 786440 | tf_op jit(solution)/shard_map/ppermute | solution.py:22
  60.7 6.9 %collective-permute-start.13 = (f32[64,1,8,128]{3,0,2,1:T(8,128)S(1)}, f32[64,1,8,128]{3,0,2,1:T(8,128)S(1)}, u32[]{:S(2)}, u32[]{:S(2)}) collective-permute-start(f32[64,1,8,128]{3,0,2,1:T(8,128)S(1)} %get-tuple-element.99), channel_id=1, source_target_pairs={{8,0},{16,8},{24,16},{32,24},{40,32},{48,40},{56,48},{64,56},{72,6... | collective-permute-start | bytes 786440 | tf_op jit(solution)/shard_map/ppermute | solution.py:23
  67.6 8.6 %collective-permute-start.14 = (f32[64,4,1,128]{3,0,2,1:T(8,128)S(1)}, f32[64,4,1,128]{3,0,2,1:T(8,128)S(1)}, u32[]{:S(2)}, u32[]{:S(2)}) collective-permute-start(f32[64,4,1,128]{3,0,2,1:T(8,128)S(1)} %get-tuple-element.50), channel_id=1, source_target_pairs={{0,1},{1,2},{2,3},{3,4},{4,5},{5,6},{6,7},{8,9},{9,10},{10,11},{11... | collective-permute-start | bytes 393224 | tf_op jit(solution)/shard_map/ppermute | solution.py:22
  72.8 8.5 %collective-permute-start.15 = (f32[64,4,1,128]{3,0,2,1:T(8,128)S(1)}, f32[64,4,1,128]{3,0,2,1:T(8,128)S(1)}, u32[]{:S(2)}, u32[]{:S(2)}) collective-permute-start(f32[64,4,1,128]{3,0,2,1:T(8,128)S(1)} %get-tuple-element.51), channel_id=1, source_target_pairs={{1,0},{2,1},{3,2},{4,3},{5,4},{6,5},{7,6},{9,8},{10,9},{11,10},{12... | collective-permute-start | bytes 393224 | tf_op jit(solution)/shard_map/ppermute | solution.py:23
  82.3 7.7 %collective-permute-start.16 = (f32[64,1,8,128]{3,0,2,1:T(8,128)S(1)}, f32[64,1,8,128]{3,0,2,1:T(8,128)S(1)}, u32[]{:S(2)}, u32[]{:S(2)}) collective-permute-start(f32[64,1,8,128]{3,0,2,1:T(8,128)S(1)} %get-tuple-element.96), channel_id=1, source_target_pairs={{0,8},{8,16},{16,24},{24,32},{32,40},{40,48},{48,56},{56,64},{64,7... | collective-permute-start | bytes 786440 | tf_op jit(solution)/shard_map/ppermute | solution.py:22
  84.2 7.5 %collective-permute-start.17 = (f32[64,1,8,128]{3,0,2,1:T(8,128)S(1)}, f32[64,1,8,128]{3,0,2,1:T(8,128)S(1)}, u32[]{:S(2)}, u32[]{:S(2)}) collective-permute-start(f32[64,1,8,128]{3,0,2,1:T(8,128)S(1)} %get-tuple-element.97), channel_id=1, source_target_pairs={{8,0},{16,8},{24,16},{32,24},{40,32},{48,40},{56,48},{64,56},{72,6... | collective-permute-start | bytes 786440 | tf_op jit(solution)/shard_map/ppermute | solution.py:23
  95.4 6.9 %collective-permute-start.19 = (f32[64,4,1,128]{3,0,2,1:T(8,128)S(1)}, f32[64,4,1,128]{3,0,2,1:T(8,128)S(1)}, u32[]{:S(2)}, u32[]{:S(2)}) collective-permute-start(f32[64,4,1,128]{3,0,2,1:T(8,128)S(1)} %get-tuple-element.49), channel_id=1, source_target_pairs={{1,0},{2,1},{3,2},{4,3},{5,4},{6,5},{7,6},{9,8},{10,9},{11,10},{12... | collective-permute-start | bytes 393224 | tf_op jit(solution)/shard_map/ppermute | solution.py:23
  103.4 7.7 %collective-permute-start.20 = (f32[64,1,8,128]{3,0,2,1:T(8,128)S(1)}, f32[64,1,8,128]{3,0,2,1:T(8,128)S(1)}, u32[]{:S(2)}, u32[]{:S(2)}) collective-permute-start(f32[64,1,8,128]{3,0,2,1:T(8,128)S(1)} %get-tuple-element.94), channel_id=1, source_target_pairs={{0,8},{8,16},{16,24},{24,32},{32,40},{40,48},{48,56},{56,64},{64,7... | collective-permute-start | bytes 786440 | tf_op jit(solution)/shard_map/ppermute | solution.py:22
  115.9 6.9 %collective-permute-start.23 = (f32[64,4,1,128]{3,0,2,1:T(8,128)S(1)}, f32[64,4,1,128]{3,0,2,1:T(8,128)S(1)}, u32[]{:S(2)}, u32[]{:S(2)}) collective-permute-start(f32[64,4,1,128]{3,0,2,1:T(8,128)S(1)} %get-tuple-element.47), channel_id=1, source_target_pairs={{1,0},{2,1},{3,2},{4,3},{5,4},{6,5},{7,6},{9,8},{10,9},{11,10},{12... | collective-permute-start | bytes 393224 | tf_op jit(solution)/shard_map/ppermute | solution.py:23
  123.8 7.7 %collective-permute-start.24 = (f32[64,1,8,128]{3,0,2,1:T(8,128)S(1)}, f32[64,1,8,128]{3,0,2,1:T(8,128)S(1)}, u32[]{:S(2)}, u32[]{:S(2)}) collective-permute-start(f32[64,1,8,128]{3,0,2,1:T(8,128)S(1)} %get-tuple-element.92), channel_id=1, source_target_pairs={{0,8},{8,16},{16,24},{24,32},{32,40},{40,48},{48,56},{56,64},{64,7... | collective-permute-start | bytes 786440 | tf_op jit(solution)/shard_map/ppermute | solution.py:22
  138.2 6.9 %collective-permute-start.27 = (f32[64,4,1,128]{3,0,2,1:T(8,128)S(1)}, f32[64,4,1,128]{3,0,2,1:T(8,128)S(1)}, u32[]{:S(2)}, u32[]{:S(2)}) collective-permute-start(f32[64,4,1,128]{3,0,2,1:T(8,128)S(1)} %get-tuple-element.45), channel_id=1, source_target_pairs={{1,0},{2,1},{3,2},{4,3},{5,4},{6,5},{7,6},{9,8},{10,9},{11,10},{12... | collective-permute-start | bytes 393224 | tf_op jit(solution)/shard_map/ppermute | solution.py:23
  146.2 7.7 %collective-permute-start.28 = (f32[64,1,8,128]{3,0,2,1:T(8,128)S(1)}, f32[64,1,8,128]{3,0,2,1:T(8,128)S(1)}, u32[]{:S(2)}, u32[]{:S(2)}) collective-permute-start(f32[64,1,8,128]{3,0,2,1:T(8,128)S(1)} %get-tuple-element.90), channel_id=1, source_target_pairs={{0,8},{8,16},{16,24},{24,32},{32,40},{40,48},{48,56},{56,64},{64,7... | collective-permute-start | bytes 786440 | tf_op jit(solution)/shard_map/ppermute | solution.py:22
  160.9 6.9 %collective-permute-start.31 = (f32[64,4,1,128]{3,0,2,1:T(8,128)S(1)}, f32[64,4,1,128]{3,0,2,1:T(8,128)S(1)}, u32[]{:S(2)}, u32[]{:S(2)}) collective-permute-start(f32[64,4,1,128]{3,0,2,1:T(8,128)S(1)} %get-tuple-element.43), channel_id=1, source_target_pairs={{1,0},{2,1},{3,2},{4,3},{5,4},{6,5},{7,6},{9,8},{10,9},{11,10},{12... | collective-permute-start | bytes 393224 | tf_op jit(solution)/shard_map/ppermute | solution.py:23
  168.8 7.7 %collective-permute-start.32 = (f32[64,1,8,128]{3,0,2,1:T(8,128)S(1)}, f32[64,1,8,128]{3,0,2,1:T(8,128)S(1)}, u32[]{:S(2)}, u32[]{:S(2)}) collective-permute-start(f32[64,1,8,128]{3,0,2,1:T(8,128)S(1)} %get-tuple-element.88), channel_id=1, source_target_pairs={{0,8},{8,16},{16,24},{24,32},{32,40},{40,48},{48,56},{56,64},{64,7... | collective-permute-start | bytes 786440 | tf_op jit(solution)/shard_map/ppermute | solution.py:22
  183.5 6.9 %collective-permute-start.35 = (f32[64,4,1,128]{3,0,2,1:T(8,128)S(1)}, f32[64,4,1,128]{3,0,2,1:T(8,128)S(1)}, u32[]{:S(2)}, u32[]{:S(2)}) collective-permute-start(f32[64,4,1,128]{3,0,2,1:T(8,128)S(1)} %get-tuple-element.41), channel_id=1, source_target_pairs={{1,0},{2,1},{3,2},{4,3},{5,4},{6,5},{7,6},{9,8},{10,9},{11,10},{12... | collective-permute-start | bytes 393224 | tf_op jit(solution)/shard_map/ppermute | solution.py:23
  191.4 7.7 %collective-permute-start.37 = (f32[64,1,8,128]{3,0,2,1:T(8,128)S(1)}, f32[64,1,8,128]{3,0,2,1:T(8,128)S(1)}, u32[]{:S(2)}, u32[]{:S(2)}) collective-permute-start(f32[64,1,8,128]{3,0,2,1:T(8,128)S(1)} %get-tuple-element.86), channel_id=1, source_target_pairs={{0,8},{8,16},{16,24},{24,32},{32,40},{40,48},{48,56},{56,64},{64,7... | collective-permute-start | bytes 786440 | tf_op jit(solution)/shard_map/ppermute | solution.py:22
  202.7 6.9 %collective-permute-start.38 = (f32[64,4,1,128]{3,0,2,1:T(8,128)S(1)}, f32[64,4,1,128]{3,0,2,1:T(8,128)S(1)}, u32[]{:S(2)}, u32[]{:S(2)}) collective-permute-start(f32[64,4,1,128]{3,0,2,1:T(8,128)S(1)} %get-tuple-element.38), channel_id=1, source_target_pairs={{1,0},{2,1},{3,2},{4,3},{5,4},{6,5},{7,6},{9,8},{10,9},{11,10},{12... | collective-permute-start | bytes 393224 | tf_op jit(solution)/shard_map/ppermute | solution.py:23
  204.0 7.1 %collective-permute-start.39 = (f32[64,4,1,128]{3,0,2,1:T(8,128)S(1)}, f32[64,4,1,128]{3,0,2,1:T(8,128)S(1)}, u32[]{:S(2)}, u32[]{:S(2)}) collective-permute-start(f32[64,4,1,128]{3,0,2,1:T(8,128)S(1)} %get-tuple-element.39), channel_id=1, source_target_pairs={{0,1},{1,2},{2,3},{3,4},{4,5},{5,6},{6,7},{8,9},{9,10},{10,11},{11... | collective-permute-start | bytes 393224 | tf_op jit(solution)/shard_map/ppermute | solution.py:22
  211.5 8.0 %collective-permute-start.41 = (f32[64,1,8,128]{3,0,2,1:T(8,128)S(1)}, f32[64,1,8,128]{3,0,2,1:T(8,128)S(1)}, u32[]{:S(2)}, u32[]{:S(2)}) collective-permute-start(f32[64,1,8,128]{3,0,2,1:T(8,128)S(1)} %get-tuple-element.82), channel_id=1, source_target_pairs={{0,8},{8,16},{16,24},{24,32},{32,40},{40,48},{48,56},{56,64},{64,7... | collective-permute-start | bytes 786440 | tf_op jit(solution)/shard_map/ppermute | solution.py:22
  223.4 7.0 %collective-permute-start.42 = (f32[64,4,1,128]{3,0,2,1:T(8,128)S(1)}, f32[64,4,1,128]{3,0,2,1:T(8,128)S(1)}, u32[]{:S(2)}, u32[]{:S(2)}) collective-permute-start(f32[64,4,1,128]{3,0,2,1:T(8,128)S(1)} %get-tuple-element.36), channel_id=1, source_target_pairs={{1,0},{2,1},{3,2},{4,3},{5,4},{6,5},{7,6},{9,8},{10,9},{11,10},{12... | collective-permute-start | bytes 393224 | tf_op jit(solution)/shard_map/ppermute | solution.py:23
  224.7 7.2 %collective-permute-start.43 = (f32[64,4,1,128]{3,0,2,1:T(8,128)S(1)}, f32[64,4,1,128]{3,0,2,1:T(8,128)S(1)}, u32[]{:S(2)}, u32[]{:S(2)}) collective-permute-start(f32[64,4,1,128]{3,0,2,1:T(8,128)S(1)} %get-tuple-element.37), channel_id=1, source_target_pairs={{0,1},{1,2},{2,3},{3,4},{4,5},{5,6},{6,7},{8,9},{9,10},{10,11},{11... | collective-permute-start | bytes 393224 | tf_op jit(solution)/shard_map/ppermute | solution.py:22
  232.3 8.3 %collective-permute-start.45 = (f32[64,1,8,128]{3,0,2,1:T(8,128)S(1)}, f32[64,1,8,128]{3,0,2,1:T(8,128)S(1)}, u32[]{:S(2)}, u32[]{:S(2)}) collective-permute-start(f32[64,1,8,128]{3,0,2,1:T(8,128)S(1)} %get-tuple-element.78), channel_id=1, source_target_pairs={{0,8},{8,16},{16,24},{24,32},{32,40},{40,48},{48,56},{56,64},{64,7... | collective-permute-start | bytes 786440 | tf_op jit(solution)/shard_map/ppermute | solution.py:22
  244.4 7.0 %collective-permute-start.46 = (f32[64,4,1,128]{3,0,2,1:T(8,128)S(1)}, f32[64,4,1,128]{3,0,2,1:T(8,128)S(1)}, u32[]{:S(2)}, u32[]{:S(2)}) collective-permute-start(f32[64,4,1,128]{3,0,2,1:T(8,128)S(1)} %get-tuple-element.34), channel_id=1, source_target_pairs={{1,0},{2,1},{3,2},{4,3},{5,4},{6,5},{7,6},{9,8},{10,9},{11,10},{12... | collective-permute-start | bytes 393224 | tf_op jit(solution)/shard_map/ppermute | solution.py:23
  245.7 7.4 %collective-permute-start.47 = (f32[64,4,1,128]{3,0,2,1:T(8,128)S(1)}, f32[64,4,1,128]{3,0,2,1:T(8,128)S(1)}, u32[]{:S(2)}, u32[]{:S(2)}) collective-permute-start(f32[64,4,1,128]{3,0,2,1:T(8,128)S(1)} %get-tuple-element.35), channel_id=1, source_target_pairs={{0,1},{1,2},{2,3},{3,4},{4,5},{5,6},{6,7},{8,9},{9,10},{10,11},{11... | collective-permute-start | bytes 393224 | tf_op jit(solution)/shard_map/ppermute | solution.py:22
  253.5 8.3 %collective-permute-start.49 = (f32[64,1,8,128]{3,0,2,1:T(8,128)S(1)}, f32[64,1,8,128]{3,0,2,1:T(8,128)S(1)}, u32[]{:S(2)}, u32[]{:S(2)}) collective-permute-start(f32[64,1,8,128]{3,0,2,1:T(8,128)S(1)} %get-tuple-element.74), channel_id=1, source_target_pairs={{0,8},{8,16},{16,24},{24,32},{32,40},{40,48},{48,56},{56,64},{64,7... | collective-permute-start | bytes 786440 | tf_op jit(solution)/shard_map/ppermute | solution.py:22
  265.6 7.0 %collective-permute-start.50 = (f32[64,4,1,128]{3,0,2,1:T(8,128)S(1)}, f32[64,4,1,128]{3,0,2,1:T(8,128)S(1)}, u32[]{:S(2)}, u32[]{:S(2)}) collective-permute-start(f32[64,4,1,128]{3,0,2,1:T(8,128)S(1)} %get-tuple-element.32), channel_id=1, source_target_pairs={{1,0},{2,1},{3,2},{4,3},{5,4},{6,5},{7,6},{9,8},{10,9},{11,10},{12... | collective-permute-start | bytes 393224 | tf_op jit(solution)/shard_map/ppermute | solution.py:23
  266.9 7.2 %collective-permute-start.51 = (f32[64,4,1,128]{3,0,2,1:T(8,128)S(1)}, f32[64,4,1,128]{3,0,2,1:T(8,128)S(1)}, u32[]{:S(2)}, u32[]{:S(2)}) collective-permute-start(f32[64,4,1,128]{3,0,2,1:T(8,128)S(1)} %get-tuple-element.33), channel_id=1, source_target_pairs={{0,1},{1,2},{2,3},{3,4},{4,5},{5,6},{6,7},{8,9},{9,10},{10,11},{11... | collective-permute-start | bytes 393224 | tf_op jit(solution)/shard_map/ppermute | solution.py:22
  274.5 8.3 %collective-permute-start.53 = (f32[64,1,8,128]{3,0,2,1:T(8,128)S(1)}, f32[64,1,8,128]{3,0,2,1:T(8,128)S(1)}, u32[]{:S(2)}, u32[]{:S(2)}) collective-permute-start(f32[64,1,8,128]{3,0,2,1:T(8,128)S(1)} %get-tuple-element.70), channel_id=1, source_target_pairs={{0,8},{8,16},{16,24},{24,32},{32,40},{40,48},{48,56},{56,64},{64,7... | collective-permute-start | bytes 786440 | tf_op jit(solution)/shard_map/ppermute | solution.py:22
  286.7 7.0 %collective-permute-start.54 = (f32[64,4,1,128]{3,0,2,1:T(8,128)S(1)}, f32[64,4,1,128]{3,0,2,1:T(8,128)S(1)}, u32[]{:S(2)}, u32[]{:S(2)}) collective-permute-start(f32[64,4,1,128]{3,0,2,1:T(8,128)S(1)} %get-tuple-element.30), channel_id=1, source_target_pairs={{1,0},{2,1},{3,2},{4,3},{5,4},{6,5},{7,6},{9,8},{10,9},{11,10},{12... | collective-permute-start | bytes 393224 | tf_op jit(solution)/shard_map/ppermute | solution.py:23
  288.0 7.2 %collective-permute-start.55 = (f32[64,4,1,128]{3,0,2,1:T(8,128)S(1)}, f32[64,4,1,128]{3,0,2,1:T(8,128)S(1)}, u32[]{:S(2)}, u32[]{:S(2)}) collective-permute-start(f32[64,4,1,128]{3,0,2,1:T(8,128)S(1)} %get-tuple-element.31), channel_id=1, source_target_pairs={{0,1},{1,2},{2,3},{3,4},{4,5},{5,6},{6,7},{8,9},{9,10},{10,11},{11... | collective-permute-start | bytes 393224 | tf_op jit(solution)/shard_map/ppermute | solution.py:22
  295.6 8.0 %collective-permute-start.57 = (f32[64,1,8,128]{3,0,2,1:T(8,128)S(1)}, f32[64,1,8,128]{3,0,2,1:T(8,128)S(1)}, u32[]{:S(2)}, u32[]{:S(2)}) collective-permute-start(f32[64,1,8,128]{3,0,2,1:T(8,128)S(1)} %get-tuple-element.66), channel_id=1, source_target_pairs={{0,8},{8,16},{16,24},{24,32},{32,40},{40,48},{48,56},{56,64},{64,7... | collective-permute-start | bytes 786440 | tf_op jit(solution)/shard_map/ppermute | solution.py:22
  307.4 7.8 %collective-permute-start.58 = (f32[64,4,1,128]{3,0,2,1:T(8,128)S(1)}, f32[64,4,1,128]{3,0,2,1:T(8,128)S(1)}, u32[]{:S(2)}, u32[]{:S(2)}) collective-permute-start(f32[64,4,1,128]{3,0,2,1:T(8,128)S(1)} %get-tuple-element.28), channel_id=1, source_target_pairs={{1,0},{2,1},{3,2},{4,3},{5,4},{6,5},{7,6},{9,8},{10,9},{11,10},{12... | collective-permute-start | bytes 393224 | tf_op jit(solution)/shard_map/ppermute | solution.py:23
  308.7 8.0 %collective-permute-start.59 = (f32[64,4,1,128]{3,0,2,1:T(8,128)S(1)}, f32[64,4,1,128]{3,0,2,1:T(8,128)S(1)}, u32[]{:S(2)}, u32[]{:S(2)}) collective-permute-start(f32[64,4,1,128]{3,0,2,1:T(8,128)S(1)} %get-tuple-element.29), channel_id=1, source_target_pairs={{0,1},{1,2},{2,3},{3,4},{4,5},{5,6},{6,7},{8,9},{9,10},{10,11},{11... | collective-permute-start | bytes 393224 | tf_op jit(solution)/shard_map/ppermute | solution.py:22
  317.2 7.7 %collective-permute-start.61 = (f32[64,1,8,128]{3,0,2,1:T(8,128)S(1)}, f32[64,1,8,128]{3,0,2,1:T(8,128)S(1)}, u32[]{:S(2)}, u32[]{:S(2)}) collective-permute-start(f32[64,1,8,128]{3,0,2,1:T(8,128)S(1)} %get-tuple-element.62), channel_id=1, source_target_pairs={{0,8},{8,16},{16,24},{24,32},{32,40},{40,48},{48,56},{56,64},{64,7... | collective-permute-start | bytes 786440 | tf_op jit(solution)/shard_map/ppermute | solution.py:22
  328.8 8.5 %collective-permute-start.62 = (f32[64,4,1,128]{3,0,2,1:T(8,128)S(1)}, f32[64,4,1,128]{3,0,2,1:T(8,128)S(1)}, u32[]{:S(2)}, u32[]{:S(2)}) collective-permute-start(f32[64,4,1,128]{3,0,2,1:T(8,128)S(1)} %get-tuple-element.26), channel_id=1, source_target_pairs={{1,0},{2,1},{3,2},{4,3},{5,4},{6,5},{7,6},{9,8},{10,9},{11,10},{12... | collective-permute-start | bytes 393224 | tf_op jit(solution)/shard_map/ppermute | solution.py:23
  330.1 8.7 %collective-permute-start.63 = (f32[64,4,1,128]{3,0,2,1:T(8,128)S(1)}, f32[64,4,1,128]{3,0,2,1:T(8,128)S(1)}, u32[]{:S(2)}, u32[]{:S(2)}) collective-permute-start(f32[64,4,1,128]{3,0,2,1:T(8,128)S(1)} %get-tuple-element.27), channel_id=1, source_target_pairs={{0,1},{1,2},{2,3},{3,4},{4,5},{5,6},{6,7},{8,9},{9,10},{10,11},{11... | collective-permute-start | bytes 393224 | tf_op jit(solution)/shard_map/ppermute | solution.py:22
  339.2 7.7 %collective-permute-start.65 = (f32[64,1,8,128]{3,0,2,1:T(8,128)S(1)}, f32[64,1,8,128]{3,0,2,1:T(8,128)S(1)}, u32[]{:S(2)}, u32[]{:S(2)}) collective-permute-start(f32[64,1,8,128]{3,0,2,1:T(8,128)S(1)} %get-tuple-element.58), channel_id=1, source_target_pairs={{0,8},{8,16},{16,24},{24,32},{32,40},{40,48},{48,56},{56,64},{64,7... | collective-permute-start | bytes 786440 | tf_op jit(solution)/shard_map/ppermute | solution.py:22
  350.7 8.5 %collective-permute-start.66 = (f32[64,4,1,128]{3,0,2,1:T(8,128)S(1)}, f32[64,4,1,128]{3,0,2,1:T(8,128)S(1)}, u32[]{:S(2)}, u32[]{:S(2)}) collective-permute-start(f32[64,4,1,128]{3,0,2,1:T(8,128)S(1)} %get-tuple-element.24), channel_id=1, source_target_pairs={{1,0},{2,1},{3,2},{4,3},{5,4},{6,5},{7,6},{9,8},{10,9},{11,10},{12... | collective-permute-start | bytes 393224 | tf_op jit(solution)/shard_map/ppermute | solution.py:23
  352.0 8.7 %collective-permute-start.67 = (f32[64,4,1,128]{3,0,2,1:T(8,128)S(1)}, f32[64,4,1,128]{3,0,2,1:T(8,128)S(1)}, u32[]{:S(2)}, u32[]{:S(2)}) collective-permute-start(f32[64,4,1,128]{3,0,2,1:T(8,128)S(1)} %get-tuple-element.25), channel_id=1, source_target_pairs={{0,1},{1,2},{2,3},{3,4},{4,5},{5,6},{6,7},{8,9},{9,10},{10,11},{11... | collective-permute-start | bytes 393224 | tf_op jit(solution)/shard_map/ppermute | solution.py:22
  (22 other events, 131.1 us)
where the time goes:
time: 474 us; the launch traced here: 470 us
  starting transfers between devices  216 us (46%)
  waiting for transfers between devices  127 us (27%)
  blocking collectives  93.5 us (20%)
  other arithmetic  23.6 us (5%)
  local copies, waits for them, and re-layouts  7.6 us (2%)
    ppermute x34, starting transfers between devices, with_halo(): before = lax.ppermute(last, axis, up)  156 us
    psum x1, blocking collectives, shards(): total_gram = lax.psum(local_gram, ('gx', 'gy'))  93.5 us
    ppermute x34, waiting for transfers between devices, with_halo(): after = lax.ppermute(initial, axis, down)  92.6 us
    ppermute x34, starting transfers between devices, with_halo(): after = lax.ppermute(initial, axis, down)  60.2 us
    ppermute x34, waiting for transfers between devices, with_halo(): before = lax.ppermute(last, axis, up)  34 us
  transfers between devices with their start and end apart: 68, of which 56 were waited for; matrix products, arithmetic and copies ran while one was open for 1% of the time, Pallas kernels for 0%

commit v1 on v0

v1 whole, which is shorter than its diff:
```python
import math

import jax
import jax.numpy as jnp
from jax import lax
from jax.experimental import pallas as pl
from jax.experimental.pallas import tpu as pltpu
from jax.sharding import Mesh, PartitionSpec as P

STEPS = 8
time_step = 0.07
prior_weight = 0.5

OWN = 8
EXT = 3 * OWN
CHUNK = 40

f32 = jnp.float32


def pack_kernel(got, first, second, half):
    for y in range(OWN):
        for j in range(8):
            row = (j // 2) * CHUNK + (j % 2) * 8 + y
            first[y, j] = got[pl.ds(row, 8, stride=4 * CHUNK)]
            second[y, j] = got[pl.ds(row + 16, 8, stride=4 * CHUNK)]
        for i in range(4):
            half[y, i] = got[pl.ds(i * CHUNK + 32 + y, 8, stride=4 * CHUNK)]


def coef_kernel(m0, m1, m2, t0, t1, t2, coef, stay):
    core = lax.axis_index("tc")
    for strip, (mine, theirs) in enumerate(((m0, t0), (m1, t1), (m2, t2))):
        for y in range(OWN):
            for i in range(4):
                for ref, j in ((mine, 2 * i + core), (theirs, 2 * i + 1 - core)):
                    a = time_step * ref[y, i]
                    coef[strip * OWN + y, j] = a
                    stay[strip * OWN + y, j] = 1.0 - 6.0 * a


def masks():
    lane = lax.broadcasted_iota(jnp.int32, (8, 128), 1)
    sub = lax.broadcasted_iota(jnp.int32, (8, 128), 0)
    return lane == 0, lane == 127, sub == 0, sub == 7


def put(buf, y, vals, m):
    for j in range(8):
        buf[y, j + 1] = vals[j]
    buf[y, 0] = jnp.where(m[2], 0.0, pltpu.roll(vals[7], 1, 0))
    buf[y, 9] = jnp.where(m[3], 0.0, pltpu.roll(vals[0], 7, 0))


def row_sums(buf, y, m):
    row = [buf[y, j] for j in range(10)]
    out = []
    for j in range(8):
        c = row[j + 1]
        up = jnp.where(m[0], 0.0, pltpu.roll(c, 1, 1))
        down = jnp.where(m[1], 0.0, pltpu.roll(c, 127, 1))
        s = (buf[y - 1, j + 1] + buf[y + 1, j + 1]) + (row[j] + row[j + 2]) + (up + down)
        out.append((c, s))
    return out


def forward_kernel(before, own, after, coef, stay, out, scaled, ping, pong):
    m = masks()
    for strip, ref in enumerate((before, own, after)):
        for y in range(OWN):
            vals = []
            for j in range(8):
                v = coef[strip * OWN + y, j] * ref[y, j]
                scaled[strip * OWN + y, j] = v
                vals.append(v)
            put(ping, strip * OWN + y, vals, m)
    bufs = (ping, pong)
    for k in range(1, STEPS):
        now, later = bufs[(k - 1) % 2], bufs[k % 2]
        for y in range(k, EXT - k):
            vals = []
            for j, (c, s) in enumerate(row_sums(now, y, m)):
                vals.append((scaled[y, j] + stay[y, j] * c) + coef[y, j] * s)
            put(later, y, vals, m)
    now = bufs[(STEPS - 1) % 2]
    for y in range(OWN, 2 * OWN):
        for j, (c, s) in enumerate(row_sums(now, y, m)):
            out[y - OWN, j] = (own[y - OWN, j] + c / coef[y, j]) + (s - 6.0 * c)


def adjoint(before, own, after, coef, stay, total, ping, pong, finish):
    m = masks()
    for strip, ref in enumerate((before, own, after)):
        for y in range(OWN):
            put(ping, strip * OWN + y, [ref[y, j] for j in range(8)], m)
    bufs = (ping, pong)
    for k in range(1, STEPS + 1):
        now, later = bufs[(k - 1) % 2], bufs[k % 2]
        for y in range(k, EXT - k):
            vals = []
            for j, (c, s) in enumerate(row_sums(now, y, m)):
                w = stay[y, j] * c + coef[y, j] * s
                vals.append(w)
                if OWN <= y < 2 * OWN:
                    i = y - OWN
                    t = (own[i, j] if k == 1 else total[i, j]) + w
                    if k < STEPS:
                        total[i, j] = t
                    else:
                        finish(i, j, t)
            if k < STEPS:
                put(later, y, vals, m)


def adjoint_first_kernel(before, own, after, coef, stay, out, total, ping, pong):
    def finish(y, j, t):
        out[y, j] = t

    adjoint(before, own, after, coef, stay, total, ping, pong, finish)


def adjoint_second_kernel(before, own, after, coef, stay, first, out, total, ping, pong):
    def row(y, j, probe):
        return pl.ds((j // 2) * 32 + probe * 16 + (j % 2) * 8 + y, 8, stride=128)

    def finish(y, j, t):
        out[row(y, j, 0)] = first[y, j]
        out[row(y, j, 1)] = t

    adjoint(before, own, after, coef, stay, total, ping, pong, finish)


def gram_kernel(back, probes, storage, flat, packed):
    for r in range(16):
        rows = pl.ds(r, 64, stride=16)
        y = (time_step * storage[r:r + 1, :]) * back[rows] + prior_weight * probes[rows]
        flat[:, r * 128:(r + 1) * 128] = y
    y = flat[...]
    gram = lax.dot_general(y, y, (((1,), (1,)), ((), ())), precision=lax.Precision.HIGHEST, preferred_element_type=f32)
    packed[...] = jnp.concatenate([gram[:32], gram[32:]], axis=1)


def solve_kernel(parts, flat, basis, factor, scale):
    dense = parts[0]
    for i in range(1, parts.shape[0]):
        dense = dense + parts[i]
    gram = jnp.concatenate([dense[:, :64], dense[:, 64:]], axis=0)
    row = lax.broadcasted_iota(jnp.int32, (64, 64), 0)
    col = lax.broadcasted_iota(jnp.int32, (64, 64), 1)
    eye = jnp.where(row == col, 1.0, 0.0)
    work = jnp.concatenate([gram, eye], axis=1)
    rows = lax.broadcasted_iota(jnp.int32, (64, 128), 0)
    diag = jnp.ones((64, 128), f32)
    for k in range(64):
        pivot_row = work[k:k + 1, :]
        column = jnp.broadcast_to(work[:, k:k + 1], (64, 128))
        pivot = column[k:k + 1, :]
        diag = jnp.where(rows == k, pivot, diag)
        work = work - jnp.where(rows > k, column * (1.0 / pivot), 0.0) * pivot_row
    work = work * lax.rsqrt(diag)
    upper = jnp.where(row <= col, work[:, :64], 0.0)
    factor[...] = upper / scale
    inverse = work[:, 64:] * scale
    solved = lax.dot_general(inverse, flat[...], (((1,), (0,)), ((), ())), precision=lax.Precision.HIGHEST, preferred_element_type=f32)
    for r in range(16):
        basis[pl.ds(r, 64, stride=16)] = solved[:, r * 128:(r + 1) * 128]


def shape(*dims):
    return jax.ShapeDtypeStruct(dims, f32)


def call(kernel, outs, *args, scratch=(), flops=0, name):
    spec = pl.BlockSpec(memory_space=pltpu.VMEM)
    many = isinstance(outs, tuple)
    moved = 4 * sum(a.size for a in args)
    return pl.pallas_call(
        kernel,
        out_shape=outs,
        in_specs=[spec] * len(args),
        out_specs=tuple([spec] * len(outs)) if many else spec,
        scratch_shapes=[pltpu.VMEM(s, f32) for s in scratch],
        compiler_params=pltpu.CompilerParams(vmem_limit_bytes=32 * 1024 * 1024),
        cost_estimate=pl.CostEstimate(flops=flops, bytes_accessed=moved, transcendentals=0),
        name=name,
    )(*args)


def shards(probes, conduct, storage):
    source = (time_step * storage[None] * probes).reshape(32, 32, 128)
    halves = jnp.broadcast_to(conduct[None], (16, 2, 8, 128)).reshape(32, 8, 128)
    got = lax.all_to_all(jnp.concatenate([source, halves], axis=1), ("ty", "tx", "tc"), 0, 0, tiled=True)
    field = shape(OWN, 8, 8, 128)
    first, second, half = call(
        pack_kernel, (field, field, shape(OWN, 4, 8, 128)), got.reshape(32 * CHUNK, 128), name="pack"
    )
    up = [(i, i + 1) for i in range(7)]
    down = [(j, i) for i, j in up]

    def sides(a):
        return lax.ppermute(a, "tz", up), a, lax.ppermute(a, "tz", down)

    def swap(a):
        return lax.ppermute(a, "tc", [(0, 1), (1, 0)])

    halfs = sides(half)
    fields = [sides(first), sides(second)]
    wide = shape(EXT, 8, 8, 128)
    coefs = call(coef_kernel, (wide, wide), *halfs, *[swap(h) for h in halfs], name="coef")
    pads = ((EXT, 10, 8, 128),) * 2
    work = 14 * 120 * 8 * 1024
    forward = [
        call(forward_kernel, field, *f, *coefs, scratch=(wide.shape,) + pads, flops=work, name="forward") for f in fields
    ]
    forward = [sides(f) for f in forward]
    scratch = (field.shape,) + pads
    total = call(adjoint_first_kernel, field, *forward[0], *coefs, scratch=scratch, flops=work, name="adjoint1")
    summed = call(adjoint_second_kernel, shape(1024, 128), *forward[1], *coefs, total, scratch=scratch, flops=work, name="adjoint2")
    back = lax.all_to_all(summed.reshape(32, 32, 128), ("ty", "tx", "tc"), 0, 0, tiled=True)
    flat, gram = call(
        gram_kernel,
        (shape(64, 2048), shape(32, 128)),
        back.reshape(1024, 128),
        probes.reshape(1024, 128),
        storage.reshape(16, 128),
        name="gram",
    )
    gram = gram + swap(gram)
    parts = lax.all_to_all(jnp.broadcast_to(gram[None], (16, 32, 128)), ("ty", "tx"), 0, 0, tiled=True)
    parts = lax.all_to_all(jnp.broadcast_to(parts.sum(0)[None], (8, 32, 128)), "tz", 0, 0, tiled=True)
    scale = math.sqrt(64 * 64 * 128)

    def solve(*refs):
        solve_kernel(*refs, scale)

    basis, factor = call(solve, (shape(1024, 128), shape(64, 64)), parts, flat, name="solve")
    return basis.reshape(probes.shape), factor


def solution(mesh):
    fine = Mesh(mesh.devices.reshape(4, 4, 2, 8), ("ty", "tx", "tc", "tz"))
    gx = ("ty", "tx", "tc")
    placed = (P(None, gx, "tz", None), P(gx, "tz", None), P(gx, "tz", None))
    return jax.shard_map(
        shards,
        mesh=fine,
        in_specs=placed,
        out_specs=(P(None, gx, "tz", None), P()),
        check_vma=False,
    )
```

time: 474 us -> 127 us (0.27)
  starting transfers between devices: 216 us -> 31.3 us
  waiting for transfers between devices: 127 us -> 10.3 us
  blocking collectives: 93.5 us -> 65.1 us
  other arithmetic: 23.6 us -> 1.87 us
  Pallas kernels: 0 us -> 17.1 us
  local copies, waits for them, and re-layouts: 7.6 us -> 0.06 us
    ppermute x68 -> x14, starting transfers between devices: 216 us -> 31.3 us  [the longest x10 30.6 us: sides(): return (lax.ppermute(a, 'tz', up), a, lax.ppermute(a, 'tz', down))]
    ppermute x68 -> x14, waiting for transfers between devices: 127 us -> 10.3 us  [the longest x10 8.11 us: sides(): return (lax.ppermute(a, 'tz', up), a, lax.ppermute(a, 'tz', down))]
    psum x1 -> x0, blocking collectives: 93.5 us -> none  [shards(): total_gram = lax.psum(local_gram, ('gx', 'gy'))]
    all_to_all x0 -> x4, blocking collectives: none -> 65.1 us  [the longest x1 19.3 us: shards(): lax.all_to_all(jnp.concatenate([source, halves], axis=1), ('ty', 'tx', 't...]
    pallas_call x0 -> x8, Pallas kernels: none -> 17.1 us  [call(): pl.pallas_call(kernel, out_shape=outs, in_specs=[spec] * len(args), out_s...]
    another operation x4 -> x0, other arithmetic: 11.4 us -> none  [the longest x3 6.52 us: shards(): upper = jnp.linalg.cholesky(total_gram).T]
    add x9 -> x1, other arithmetic: 5.27 us -> 0.01 us  [shards(): gram = gram + swap(gram)]
    slice x34 -> x0, local copies, waits for them, and re-layouts: 4.79 us -> none  [the longest x16 3.36 us: laplace_inner(): above = jnp.concatenate([centre[..., 1:], zero_plane], axis=3)]
  transfers between devices with their start and end apart: 68 -> 14, of which waited for: 56 -> 6; matrix products, arithmetic and copies ran while one was open for 1% -> 0% of each run, Pallas kernels for 0% -> 5%
where the time goes in v1:
time: 127 us
  blocking collectives  65.1 us (51%)
  starting transfers between devices  31.3 us (25%)
  Pallas kernels  17.1 us (13%)
  waiting for transfers between devices  10.3 us (8%)
  other arithmetic  1.87 us (1%)
    ppermute x10, starting transfers between devices, sides(): return (lax.ppermute(a, 'tz', up), a, lax.ppermute(a, 'tz', down))  30.6 us
    all_to_all x1, blocking collectives, shards(): lax.all_to_all(jnp.concatenate([source, halves], axis=1), ('ty', 'tx', 't...  19.3 us
    all_to_all x1, blocking collectives, shards(): lax.all_to_all(jnp.broadcast_to(parts.sum(0)[None], (8, 32, 128)), 'tz',...  18.1 us
    pallas_call x8, Pallas kernels, call(): pl.pallas_call(kernel, out_shape=outs, in_specs=[spec] * len(args), out_s...  17.1 us
    all_to_all x1, blocking collectives, shards(): lax.all_to_all(summed.reshape(32, 32, 128), ('ty', 'tx', 'tc'), 0, 0, til...  15.4 us
    all_to_all x1, blocking collectives, shards(): lax.all_to_all(jnp.broadcast_to(gram[None], (16, 32, 128)), ('ty', 'tx'),...  12.3 us
    ppermute x10, waiting for transfers between devices, sides(): return (lax.ppermute(a, 'tz', up), a, lax.ppermute(a, 'tz', down))  8.11 us
  transfers between devices with their start and end apart: 14, of which 6 were waited for; matrix products, arithmetic and copies ran while one was open for 0% of the time, Pallas kernels for 5%

profile of v1, /device:TPU:2, one launch (start us, length us, event | category | flops | bytes accessed | tf_op | source)
XLA Modules:
  0.0 126.5 jit_solution(14517332414205909861)
XLA Ops:
  0.6 0.7 broadcast_multiply_fusion.1
  1.3 0.0 copy-start.2
  1.3 1.1 broadcast_multiply_fusion
  2.4 0.0 copy-done.2
  2.5 19.3 %all_to_all.20 = f32[32,40,128]{2,1,0:T(8,128)S(1)} all-to-all(f32[32,40,128]{2,1,0:T(8,128)S(1)} %pad_maximum_fusion), channel_id=1, replica_groups=mesh['ty'=4,'tx'=4,'tc'=2,'tz'=8] {'ty','tx','tc'}, dimensions={0} | all-to-all | bytes 1310720 | tf_op jit(solution)/shard_map/all_to_all | solution.py:192
  21.8 0.4 pack.1
  22.2 3.8 %collective-permute-start.2 = (f32[8,4,8,128]{3,2,1,0:T(8,128)S(1)}, f32[8,4,8,128]{3,2,1,0:T(8,128)S(1)}, u32[]{:S(2)}, u32[]{:S(2)}) collective-permute-start(f32[8,4,8,128]{3,2,1,0:T(8,128)S(1)} %get-tuple-element.12.m1), channel_id=1, source_target_pairs={{0,1},{1,2},{2,3},{3,4},{4,5},{5,6},{6,7},{8,9},{9,10},{10,11},{11... | collective-permute-start | bytes 393224 | tf_op jit(solution)/shard_map/ppermute | solution.py:201
  26.1 1.3 %collective-permute-start.3 = (f32[8,4,8,128]{3,2,1,0:T(8,128)S(1)}, f32[8,4,8,128]{3,2,1,0:T(8,128)S(1)}, u32[]{:S(2)}, u32[]{:S(2)}) collective-permute-start(f32[8,4,8,128]{3,2,1,0:T(8,128)S(1)} %get-tuple-element.12.m1), channel_id=1, source_target_pairs={{1,0},{2,1},{3,2},{4,3},{5,4},{6,5},{7,6},{9,8},{10,9},{11,10},{12... | collective-permute-start | bytes 393224 | tf_op jit(solution)/shard_map/ppermute | solution.py:201
  27.4 0.1 collective-permute-start.5
  27.5 1.8 %collective-permute-done.2.m0 = f32[8,4,8,128]{3,2,1,0:T(8,128)S(1)} collective-permute-done((f32[8,4,8,128]{3,2,1,0:T(8,128)S(1)}, f32[8,4,8,128]{3,2,1,0:T(8,128)S(1)}, u32[]{:S(2)}, u32[]{:S(2)}) %collective-permute-start.2) | collective-permute-done | bytes 131104 | tf_op jit(solution)/shard_map/ppermute | solution.py:201
  29.3 0.0 collective-permute-start.4
  29.3 1.3 %collective-permute-start.10 = (f32[8,8,8,128]{3,2,1,0:T(8,128)S(1)}, f32[8,8,8,128]{3,2,1,0:T(8,128)S(1)}, u32[]{:S(2)}, u32[]{:S(2)}) collective-permute-start(f32[8,8,8,128]{3,2,1,0:T(8,128)S(1)} %get-tuple-element.15.own), channel_id=1, source_target_pairs={{1,0},{2,1},{3,2},{4,3},{5,4},{6,5},{7,6},{9,8},{10,9},{11,10},{12... | collective-permute-start | bytes 786440 | tf_op jit(solution)/shard_map/ppermute | solution.py:201
  30.6 5.0 %collective-permute-start.9 = (f32[8,8,8,128]{3,2,1,0:T(8,128)S(1)}, f32[8,8,8,128]{3,2,1,0:T(8,128)S(1)}, u32[]{:S(2)}, u32[]{:S(2)}) collective-permute-start(f32[8,8,8,128]{3,2,1,0:T(8,128)S(1)} %get-tuple-element.15.own), channel_id=1, source_target_pairs={{0,1},{1,2},{2,3},{3,4},{4,5},{5,6},{6,7},{8,9},{9,10},{10,11},{11... | collective-permute-start | bytes 786440 | tf_op jit(solution)/shard_map/ppermute | solution.py:201
  35.6 0.0 collective-permute-done.3.m2
  35.6 3.9 %collective-permute-start = (f32[8,8,8,128]{3,2,1,0:T(8,128)S(1)}, f32[8,8,8,128]{3,2,1,0:T(8,128)S(1)}, u32[]{:S(2)}, u32[]{:S(2)}) collective-permute-start(f32[8,8,8,128]{3,2,1,0:T(8,128)S(1)} %get-tuple-element.11.own), channel_id=1, source_target_pairs={{0,1},{1,2},{2,3},{3,4},{4,5},{5,6},{6,7},{8,9},{9,10},{10,11},{11... | collective-permute-start | bytes 786440 | tf_op jit(solution)/shard_map/ppermute | solution.py:201
  39.5 0.0 collective-permute-done.5.t1
  39.5 1.3 %collective-permute-start.1 = (f32[8,8,8,128]{3,2,1,0:T(8,128)S(1)}, f32[8,8,8,128]{3,2,1,0:T(8,128)S(1)}, u32[]{:S(2)}, u32[]{:S(2)}) collective-permute-start(f32[8,8,8,128]{3,2,1,0:T(8,128)S(1)} %get-tuple-element.11.own), channel_id=1, source_target_pairs={{1,0},{2,1},{3,2},{4,3},{5,4},{6,5},{7,6},{9,8},{10,9},{11,10},{12... | collective-permute-start | bytes 786440 | tf_op jit(solution)/shard_map/ppermute | solution.py:201
  40.8 0.0 collective-permute-done.4.t0
  40.9 0.1 collective-permute-start.6
  41.0 1.3 %collective-permute-done.6.t2 = f32[8,4,8,128]{3,2,1,0:T(8,128)S(1)} collective-permute-done((f32[8,4,8,128]{3,2,1,0:T(8,128)S(1)}, f32[8,4,8,128]{3,2,1,0:T(8,128)S(1)}, u32[]{:S(2)}, u32[]{:S(2)}) %collective-permute-start.6) | collective-permute-done | bytes 131104 | tf_op jit(solution)/shard_map/ppermute | solution.py:204
  42.3 0.1 coef.1
  42.4 0.0 collective-permute-done.10.after
  42.4 0.0 collective-permute-done.9.before
  42.4 2.1 %forward.3.own = f32[8,8,8,128]{3,2,1,0:T(8,128)S(1)} custom-call(f32[8,8,8,128]{3,2,1,0:T(8,128)S(1)} %collective-permute-done.9.before, f32[8,8,8,128]{3,2,1,0:T(8,128)S(1)} %get-tuple-element.15.own, f32[8,8,8,128]{3,2,1,0:T(8,128)S(1)} %collective-permute-done.10.after, f32[24,8,8,128]{3,2,1,0:T(8,128)S(1)} %get-tuple-element.13.coef, ...), custom_call_target="tpu_custom_call" | custom-call | flops 13762560 | bytes 2359296 | tf_op jit(solution)/shard_map/forward/pallas_call | solution.py:177
  44.6 5.0 %collective-permute-start.11 = (f32[8,8,8,128]{3,2,1,0:T(8,128)S(1)}, f32[8,8,8,128]{3,2,1,0:T(8,128)S(1)}, u32[]{:S(2)}, u32[]{:S(2)}) collective-permute-start(f32[8,8,8,128]{3,2,1,0:T(8,128)S(1)} %forward.3.own), channel_id=1, source_target_pairs={{0,1},{1,2},{2,3},{3,4},{4,5},{5,6},{6,7},{8,9},{9,10},{10,11},{11... | collective-permute-start | bytes 786440 | tf_op jit(solution)/shard_map/ppermute | solution.py:201
  49.6 1.3 %collective-permute-start.12 = (f32[8,8,8,128]{3,2,1,0:T(8,128)S(1)}, f32[8,8,8,128]{3,2,1,0:T(8,128)S(1)}, u32[]{:S(2)}, u32[]{:S(2)}) collective-permute-start(f32[8,8,8,128]{3,2,1,0:T(8,128)S(1)} %forward.3.own), channel_id=1, source_target_pairs={{1,0},{2,1},{3,2},{4,3},{5,4},{6,5},{7,6},{9,8},{10,9},{11,10},{12... | collective-permute-start | bytes 786440 | tf_op jit(solution)/shard_map/ppermute | solution.py:201
  50.9 0.0 collective-permute-done.before
  50.9 0.0 collective-permute-done.1.after
  50.9 2.1 %forward.2.own = f32[8,8,8,128]{3,2,1,0:T(8,128)S(1)} custom-call(f32[8,8,8,128]{3,2,1,0:T(8,128)S(1)} %collective-permute-done.before, f32[8,8,8,128]{3,2,1,0:T(8,128)S(1)} %get-tuple-element.11.own, f32[8,8,8,128]{3,2,1,0:T(8,128)S(1)} %collective-permute-done.1.after, f32[24,8,8,128]{3,2,1,0:T(8,128)S(1)} %get-tuple-element.13.coef, ...), custom_call_target="tpu_custom_call" | custom-call | flops 13762560 | bytes 2359296 | tf_op jit(solution)/shard_map/forward/pallas_call | solution.py:177
  53.1 6.2 %collective-permute-start.7 = (f32[8,8,8,128]{3,2,1,0:T(8,128)S(1)}, f32[8,8,8,128]{3,2,1,0:T(8,128)S(1)}, u32[]{:S(2)}, u32[]{:S(2)}) collective-permute-start(f32[8,8,8,128]{3,2,1,0:T(8,128)S(1)} %forward.2.own), channel_id=1, source_target_pairs={{0,1},{1,2},{2,3},{3,4},{4,5},{5,6},{6,7},{8,9},{9,10},{10,11},{11... | collective-permute-start | bytes 786440 | tf_op jit(solution)/shard_map/ppermute | solution.py:201
  59.3 1.5 %collective-permute-start.8 = (f32[8,8,8,128]{3,2,1,0:T(8,128)S(1)}, f32[8,8,8,128]{3,2,1,0:T(8,128)S(1)}, u32[]{:S(2)}, u32[]{:S(2)}) collective-permute-start(f32[8,8,8,128]{3,2,1,0:T(8,128)S(1)} %forward.2.own), channel_id=1, source_target_pairs={{1,0},{2,1},{3,2},{4,3},{5,4},{6,5},{7,6},{9,8},{10,9},{11,10},{12... | collective-permute-start | bytes 786440 | tf_op jit(solution)/shard_map/ppermute | solution.py:201
  60.8 0.0 collective-permute-done.11.before
  60.8 0.7 collective-permute-done.12.after
  61.5 2.2 %adjoint1.1.first = f32[8,8,8,128]{3,2,1,0:T(8,128)S(1)} custom-call(f32[8,8,8,128]{3,2,1,0:T(8,128)S(1)} %collective-permute-done.11.before, f32[8,8,8,128]{3,2,1,0:T(8,128)S(1)} %forward.3.own, f32[8,8,8,128]{3,2,1,0:T(8,128)S(1)} %collective-permute-done.12.after, f32[24,8,8,128]{3,2,1,0:T(8,128)S(1)} %get-tuple-element.13.coef, ...), custom_call_target="tpu_custom_call" | custom-call | flops 13762560 | bytes 2359296 | tf_op jit(solution)/shard_map/adjoint1/pallas_call | solution.py:177
  63.7 1.2 collective-permute-done.7.before
  64.9 4.4 %collective-permute-done.8.after = f32[8,8,8,128]{3,2,1,0:T(8,128)S(1)} collective-permute-done((f32[8,8,8,128]{3,2,1,0:T(8,128)S(1)}, f32[8,8,8,128]{3,2,1,0:T(8,128)S(1)}, u32[]{:S(2)}, u32[]{:S(2)}) %collective-permute-start.8) | collective-permute-done | bytes 262176 | tf_op jit(solution)/shard_map/ppermute | solution.py:201
  69.3 2.4 %adjoint2.1 = f32[1024,128]{1,0:T(8,128)S(1)} custom-call(f32[8,8,8,128]{3,2,1,0:T(8,128)S(1)} %collective-permute-done.7.before, f32[8,8,8,128]{3,2,1,0:T(8,128)S(1)} %forward.2.own, f32[8,8,8,128]{3,2,1,0:T(8,128)S(1)} %collective-permute-done.8.after, f32[24,8,8,128]{3,2,1,0:T(8,128)S(1)} %get-tuple-element.13.coef, ...), custom_call_target="tpu_custom_call" | custom-call | flops 13762560 | bytes 2621440 | tf_op jit(solution)/shard_map/adjoint2/pallas_call | solution.py:177
  71.7 0.0 copy-start
  71.7 0.0 copy-start.1
  71.7 15.4 %all_to_all.21 = f32[32,32,128]{2,1,0:T(8,128)S(1)} all-to-all(f32[32,32,128]{2,1,0:T(8,128)S(1)} %bitcast.11), channel_id=1, replica_groups=mesh['ty'=4,'tx'=4,'tc'=2,'tz'=8] {'ty','tx','tc'}, dimensions={0} | all-to-all | bytes 1048576 | tf_op jit(solution)/shard_map/all_to_all | solution.py:219
  87.1 0.0 copy-done
  87.1 0.0 copy-done.1
  87.1 0.8 gram.1
  87.9 0.4 collective-permute-start.13
  88.3 0.8 collective-permute-done.13
  89.2 12.3 %all_to_all.22 = f32[16,32,128]{2,1,0:T(8,128)S(1)} all-to-all(f32[16,32,128]{2,1,0:T(8,128)S(1)} %broadcast_in_dim.7), channel_id=1, replica_groups=mesh['ty'=4,'tx'=4,'tc'=2,'tz'=8] {'ty','tx'}, dimensions={0} | all-to-all | bytes 524288 | tf_op jit(solution)/shard_map/all_to_all | solution.py:229
  101.5 18.1 %all_to_all.23.refs_0_ = f32[8,32,128]{2,1,0:T(8,128)S(1)} all-to-all(f32[8,32,128]{2,1,0:T(8,128)S(1)} %broadcast_in_dim.8), channel_id=1, replica_groups=mesh['ty'=4,'tx'=4,'tc'=2,'tz'=8] {'tz'}, dimensions={0} | all-to-all | bytes 262144 | tf_op jit(solution)/shard_map/all_to_all | solution.py:230
  119.6 6.9 %solve.1 = (f32[1024,128]{1,0:T(8,128)}, f32[64,64]{1,0:T(8,128)}) custom-call(f32[8,32,128]{2,1,0:T(8,128)S(1)} %all_to_all.23.refs_0_, f32[64,2048]{1,0:T(8,128)S(1)} %get-tuple-element.17.refs_1_), custom_call_target="tpu_custom_call" | custom-call | bytes 655360 | tf_op jit(solution)/shard_map/solve/pallas_call | solution.py:177
  (6 shorter events, 0.1 us)
Async XLA Ops:
  1.3 1.1 copy-start.2
  22.2 7.0 %collective-permute-start.2 = (f32[8,4,8,128]{3,2,1,0:T(8,128)S(1)}, f32[8,4,8,128]{3,2,1,0:T(8,128)S(1)}, u32[]{:S(2)}, u32[]{:S(2)}) collective-permute-start(f32[8,4,8,128]{3,2,1,0:T(8,128)S(1)} %get-tuple-element.12.m1), channel_id=1, source_target_pairs={{0,1},{1,2},{2,3},{3,4},{4,5},{5,6},{6,7},{8,9},{9,10},{10,11},{11... | collective-permute-start | bytes 393224 | tf_op jit(solution)/shard_map/ppermute | solution.py:201
  26.1 9.5 %collective-permute-start.3 = (f32[8,4,8,128]{3,2,1,0:T(8,128)S(1)}, f32[8,4,8,128]{3,2,1,0:T(8,128)S(1)}, u32[]{:S(2)}, u32[]{:S(2)}) collective-permute-start(f32[8,4,8,128]{3,2,1,0:T(8,128)S(1)} %get-tuple-element.12.m1), channel_id=1, source_target_pairs={{1,0},{2,1},{3,2},{4,3},{5,4},{6,5},{7,6},{9,8},{10,9},{11,10},{12... | collective-permute-start | bytes 393224 | tf_op jit(solution)/shard_map/ppermute | solution.py:201
  27.4 12.2 %collective-permute-start.5 = (f32[8,4,8,128]{3,2,1,0:T(8,128)S(1)}, f32[8,4,8,128]{3,2,1,0:T(8,128)S(1)}, u32[]{:S(2)}, u32[]{:S(2)}) collective-permute-start(f32[8,4,8,128]{3,2,1,0:T(8,128)S(1)} %get-tuple-element.12.m1), channel_id=1, source_target_pairs={{0,8},{8,0},{1,9},{9,1},{2,10},{10,2},{3,11},{11,3},{4,12},{12,4},... | collective-permute-start | bytes 393224 | tf_op jit(solution)/shard_map/ppermute | solution.py:204
  29.3 11.6 %collective-permute-start.4 = (f32[8,4,8,128]{3,2,1,0:T(8,128)S(1)}, f32[8,4,8,128]{3,2,1,0:T(8,128)S(1)}, u32[]{:S(2)}, u32[]{:S(2)}) collective-permute-start(f32[8,4,8,128]{3,2,1,0:T(8,128)S(1)} %collective-permute-done.2.m0), channel_id=1, source_target_pairs={{0,8},{8,0},{1,9},{9,1},{2,10},{10,2},{3,11},{11,3},{4,12},{12,4},... | collective-permute-start | bytes 393224 | tf_op jit(solution)/shard_map/ppermute | solution.py:204
  29.3 13.2 %collective-permute-start.10 = (f32[8,8,8,128]{3,2,1,0:T(8,128)S(1)}, f32[8,8,8,128]{3,2,1,0:T(8,128)S(1)}, u32[]{:S(2)}, u32[]{:S(2)}) collective-permute-start(f32[8,8,8,128]{3,2,1,0:T(8,128)S(1)} %get-tuple-element.15.own), channel_id=1, source_target_pairs={{1,0},{2,1},{3,2},{4,3},{5,4},{6,5},{7,6},{9,8},{10,9},{11,10},{12... | collective-permute-start | bytes 786440 | tf_op jit(solution)/shard_map/ppermute | solution.py:201
  30.6 11.9 %collective-permute-start.9 = (f32[8,8,8,128]{3,2,1,0:T(8,128)S(1)}, f32[8,8,8,128]{3,2,1,0:T(8,128)S(1)}, u32[]{:S(2)}, u32[]{:S(2)}) collective-permute-start(f32[8,8,8,128]{3,2,1,0:T(8,128)S(1)} %get-tuple-element.15.own), channel_id=1, source_target_pairs={{0,1},{1,2},{2,3},{3,4},{4,5},{5,6},{6,7},{8,9},{9,10},{10,11},{11... | collective-permute-start | bytes 786440 | tf_op jit(solution)/shard_map/ppermute | solution.py:201
  35.6 15.3 %collective-permute-start = (f32[8,8,8,128]{3,2,1,0:T(8,128)S(1)}, f32[8,8,8,128]{3,2,1,0:T(8,128)S(1)}, u32[]{:S(2)}, u32[]{:S(2)}) collective-permute-start(f32[8,8,8,128]{3,2,1,0:T(8,128)S(1)} %get-tuple-element.11.own), channel_id=1, source_target_pairs={{0,1},{1,2},{2,3},{3,4},{4,5},{5,6},{6,7},{8,9},{9,10},{10,11},{11... | collective-permute-start | bytes 786440 | tf_op jit(solution)/shard_map/ppermute | solution.py:201
  39.5 11.4 %collective-permute-start.1 = (f32[8,8,8,128]{3,2,1,0:T(8,128)S(1)}, f32[8,8,8,128]{3,2,1,0:T(8,128)S(1)}, u32[]{:S(2)}, u32[]{:S(2)}) collective-permute-start(f32[8,8,8,128]{3,2,1,0:T(8,128)S(1)} %get-tuple-element.11.own), channel_id=1, source_target_pairs={{1,0},{2,1},{3,2},{4,3},{5,4},{6,5},{7,6},{9,8},{10,9},{11,10},{12... | collective-permute-start | bytes 786440 | tf_op jit(solution)/shard_map/ppermute | solution.py:201
  40.9 1.4 %collective-permute-start.6 = (f32[8,4,8,128]{3,2,1,0:T(8,128)S(1)}, f32[8,4,8,128]{3,2,1,0:T(8,128)S(1)}, u32[]{:S(2)}, u32[]{:S(2)}) collective-permute-start(f32[8,4,8,128]{3,2,1,0:T(8,128)S(1)} %collective-permute-done.3.m2), channel_id=1, source_target_pairs={{0,8},{8,0},{1,9},{9,1},{2,10},{10,2},{3,11},{11,3},{4,12},{12,4},... | collective-permute-start | bytes 393224 | tf_op jit(solution)/shard_map/ppermute | solution.py:204
  44.6 16.2 %collective-permute-start.11 = (f32[8,8,8,128]{3,2,1,0:T(8,128)S(1)}, f32[8,8,8,128]{3,2,1,0:T(8,128)S(1)}, u32[]{:S(2)}, u32[]{:S(2)}) collective-permute-start(f32[8,8,8,128]{3,2,1,0:T(8,128)S(1)} %forward.3.own), channel_id=1, source_target_pairs={{0,1},{1,2},{2,3},{3,4},{4,5},{5,6},{6,7},{8,9},{9,10},{10,11},{11... | collective-permute-start | bytes 786440 | tf_op jit(solution)/shard_map/ppermute | solution.py:201
  49.6 11.9 %collective-permute-start.12 = (f32[8,8,8,128]{3,2,1,0:T(8,128)S(1)}, f32[8,8,8,128]{3,2,1,0:T(8,128)S(1)}, u32[]{:S(2)}, u32[]{:S(2)}) collective-permute-start(f32[8,8,8,128]{3,2,1,0:T(8,128)S(1)} %forward.3.own), channel_id=1, source_target_pairs={{1,0},{2,1},{3,2},{4,3},{5,4},{6,5},{7,6},{9,8},{10,9},{11,10},{12... | collective-permute-start | bytes 786440 | tf_op jit(solution)/shard_map/ppermute | solution.py:201
  53.1 11.8 %collective-permute-start.7 = (f32[8,8,8,128]{3,2,1,0:T(8,128)S(1)}, f32[8,8,8,128]{3,2,1,0:T(8,128)S(1)}, u32[]{:S(2)}, u32[]{:S(2)}) collective-permute-start(f32[8,8,8,128]{3,2,1,0:T(8,128)S(1)} %forward.2.own), channel_id=1, source_target_pairs={{0,1},{1,2},{2,3},{3,4},{4,5},{5,6},{6,7},{8,9},{9,10},{10,11},{11... | collective-permute-start | bytes 786440 | tf_op jit(solution)/shard_map/ppermute | solution.py:201
  59.3 10.0 %collective-permute-start.8 = (f32[8,8,8,128]{3,2,1,0:T(8,128)S(1)}, f32[8,8,8,128]{3,2,1,0:T(8,128)S(1)}, u32[]{:S(2)}, u32[]{:S(2)}) collective-permute-start(f32[8,8,8,128]{3,2,1,0:T(8,128)S(1)} %forward.2.own), channel_id=1, source_target_pairs={{1,0},{2,1},{3,2},{4,3},{5,4},{6,5},{7,6},{9,8},{10,9},{11,10},{12... | collective-permute-start | bytes 786440 | tf_op jit(solution)/shard_map/ppermute | solution.py:201
  71.7 15.4 %copy-start = (f32[64,2,8,128]{3,2,1,0:T(8,128)S(1)}, f32[64,2,8,128]{3,2,1,0:T(8,128)}, u32[]{:S(2)}) copy-start(f32[64,2,8,128]{3,2,1,0:T(8,128)} %param.3) | copy-start | bytes 1572868
  71.7 15.4 %copy-start.1 = (f32[2,8,128]{2,1,0:T(8,128)S(1)}, f32[2,8,128]{2,1,0:T(8,128)}, u32[]{:S(2)}) copy-start(f32[2,8,128]{2,1,0:T(8,128)} %param.5) | copy-start | bytes 24580
  87.9 1.2 collective-permute-start.13
